TPU v7x, 512 devices: a whole 4x4x16 slice. The times are simulated.
512 devices in a mesh: dp: 128 (over z, x, core), grp: 4 (over y).
Axes of the slice: x: 4, y: 4, z: 16, core: 2. Of those that a mesh axis runs over, the one named last changes fastest.
Arguments:
- queries: bfloat16 [32768, 4096], P('dp', 'grp'), may hold values from -6 to 6
- passages: bfloat16 [256, 128, 4096], P(None, 'dp', 'grp'), may hold values from -6 to 6
- block_lists: int32 [256, 3], P('dp'), may hold values from 0 to 255
- list_lengths: int32 [256], P('dp'), may hold values from 1 to 3, as said below
- positive: int32 [32768], P('dp'), may hold values from 0 to 32767, as said below
- loss_grad: float32 [32768], P('dp'), may hold values from -16 to 16
Outputs:
- losses: float32 [32768], P('dp')
- grad_queries: bfloat16 [32768, 4096], P('dp', 'grp')
- grad_passages: bfloat16 [256, 128, 4096], P(None, 'dp', 'grp')
Inputs may be any that keep to these rules, and one draw needn't show every extreme that they name: `block_lists`: entries of a list past its length are ignored. `list_lengths`: the 2 query blocks of one dp index list 4 blocks or fewer together; in every draw some dp index lists exactly 4, with one of its blocks listing 3. positive[q] = n * 128 + r with r == q // 256.
All inputs are finite; a program needn't handle non-finite values.
Results may differ from a plain program's by a relative error of at most 0.0052.
Values may be sent and summed in bfloat16 or wider, within the bound.
A program may use at most 64 MiB of HBM per device.

v0:
```python
import math

import jax
import jax.numpy as jnp
from jax import lax
from jax.sharding import PartitionSpec as P

D = 4096


def pick_rows(selector, table):
    return jnp.sum(jnp.where(selector[:, :, None], table[None], 0.0), axis=1)


def per_device(queries, passages, block_lists, list_lengths, positive, loss_grad):
    score_scale = 3.0 / math.sqrt(D)
    dp_count = lax.axis_size("dp")
    dp_owner = lax.axis_index("dp")
    block_count, list_cap = block_lists.shape
    block_total, shard_rows, feature_width = passages.shape
    block_size = shard_rows * dp_count
    query_rows = queries.shape[0]
    query_blocks = queries.reshape(block_count, block_size, feature_width)
    entry_index = jnp.arange(list_cap, dtype=jnp.int32)
    block_index = jnp.arange(block_count, dtype=jnp.int32)
    slot_count = block_count * list_cap
    slot_block = jnp.repeat(block_index, list_cap)
    slot_ids = block_lists.reshape(slot_count)
    slot_live = (entry_index[None, :] < list_lengths[:, None]).reshape(slot_count)
    all_ids = lax.all_gather(slot_ids, "dp", axis=0, tiled=True)
    outgoing = passages[all_ids].reshape(dp_count, slot_count, shard_rows, feature_width)
    fetched = lax.all_to_all(outgoing, "dp", split_axis=0, concat_axis=2, tiled=True).reshape(
        slot_count, block_size, feature_width
    )
    local_rows = passages.reshape(block_total * shard_rows, feature_width)
    block_match = slot_block[:, None] == block_index[None, :]
    chosen = jnp.einsum(
        "sb,bqf->sqf",
        block_match.astype(jnp.bfloat16),
        query_blocks,
        preferred_element_type=jnp.float32,
    ).astype(jnp.bfloat16)
    part_in = lax.dot_general(
        queries, local_rows, (((1,), (1,)), ((), ())), preferred_element_type=jnp.float32
    )
    part_list = jnp.einsum("sqf,spf->sqp", chosen, fetched, preferred_element_type=jnp.float32)
    full_in, full_list = lax.psum((part_in, part_list), "grp")
    scores_in = score_scale * full_in
    scores_list = score_scale * full_list
    slot_open = block_match & slot_live[:, None]
    slot_peak = jnp.max(scores_list, axis=2)
    list_peak = jnp.max(
        jnp.where(slot_open[:, :, None], slot_peak[:, None, :], -jnp.inf), axis=0
    ).reshape(query_rows)
    row_peak = jnp.maximum(jnp.max(scores_in, axis=1), list_peak)
    slot_shift = pick_rows(block_match, row_peak.reshape(block_count, block_size))
    slot_sums = jnp.sum(jnp.exp(scores_list - slot_shift[:, :, None]), axis=2)
    list_total = jnp.sum(
        jnp.where(slot_open[:, :, None], slot_sums[:, None, :], 0.0), axis=0
    ).reshape(query_rows)
    row_total = jnp.sum(jnp.exp(scores_in - row_peak[:, None]), axis=1) + list_total
    log_total = row_peak + jnp.log(row_total)
    pos_column = positive // block_size * shard_rows + positive % block_size - dp_owner * shard_rows
    column_index = jnp.arange(block_total * shard_rows, dtype=jnp.int32)
    is_positive = column_index[None, :] == pos_column[:, None]
    positive_score = jnp.sum(jnp.where(is_positive, scores_in, 0.0), axis=1)
    losses = log_total - positive_score
    weights_in = (
        loss_grad[:, None]
        * (jnp.exp(scores_in - log_total[:, None]) - is_positive.astype(jnp.float32))
    ).astype(jnp.bfloat16)
    slot_log = pick_rows(block_match, log_total.reshape(block_count, block_size))
    slot_grad = pick_rows(block_match, loss_grad.reshape(block_count, block_size))
    weights_list = jnp.where(
        slot_live[:, None, None],
        slot_grad[:, :, None] * jnp.exp(scores_list - slot_log[:, :, None]),
        0.0,
    ).astype(jnp.bfloat16)
    near_terms = jnp.dot(weights_in, local_rows, preferred_element_type=jnp.float32)
    per_slot = jnp.einsum("sqp,spf->sqf", weights_list, fetched, preferred_element_type=jnp.float32)
    far_terms = jnp.einsum(
        "sb,sqf->bqf", block_match.astype(jnp.float32), per_slot, precision=lax.Precision.HIGHEST
    ).reshape(query_rows, feature_width)
    grad_queries = (score_scale * (near_terms + far_terms)).astype(jnp.bfloat16)
    shares = (
        score_scale
        * jnp.einsum("sqp,sqf->spf", weights_list, chosen, preferred_element_type=jnp.float32)
    ).astype(jnp.bfloat16)
    returned = lax.all_to_all(
        shares.reshape(1, slot_count, block_size, feature_width),
        "dp",
        split_axis=2,
        concat_axis=0,
        tiled=True,
    )
    own_part = score_scale * lax.dot_general(
        weights_in, queries, (((0,), (0,)), ((), ())), preferred_element_type=jnp.float32
    )
    summed = (
        own_part.reshape(block_total, shard_rows, feature_width)
        .at[all_ids]
        .add(returned.reshape(dp_count * slot_count, shard_rows, feature_width).astype(jnp.float32))
    )
    return (losses, grad_queries, summed.astype(jnp.bfloat16))


def solution(mesh):
    in_specs = (P("dp", "grp"), P(None, "dp", "grp"), P("dp", None), P("dp"), P("dp"), P("dp"))
    out_specs = (P("dp"), P("dp", "grp"), P(None, "dp", "grp"))
    return jax.shard_map(
        per_device, mesh=mesh, in_specs=in_specs, out_specs=out_specs, check_vma=False
    )
```

profile of v0, /device:TPU:1, one launch (start us, length us, event | category | flops | bytes accessed | tf_op | source)
XLA Modules:
  0.0 368.8 jit_solution(769956629884457869)
XLA Ops:
  8.0 1.3 dynamic-slice
  10.2 30.3 %all-reduce = s32[768]{0:T(1024)S(1)} all-reduce(s32[768]{0:T(1024)S(1)} %dynamic-update-slice), channel_id=1, replica_groups=mesh['dp'=128,'grp'=4] {'dp'}, use_global_device_ids=true, to_apply=%add | all-reduce | flops 768 | bytes 6144
  40.5 4.9 %gather_fusion = bf16[768,1024]{1,0:T(8,128)(2,1)S(1)} fusion(bf16[256,1024]{1,0:T(8,128)(2,1)} %bitcast.57, s32[1024]{0:T(1024)S(1)} %pad_clamp_fusion), kind=kCustom, calls=%fused_computation | custom fusion | bytes 3148800 | tf_op jit(solution)/shard_map/gather | solution.py:31
  45.4 1.6 reshape.196
  47.0 13.5 %all-to-all-start = ((bf16[128,6,1,1024]{3,1,2,0:T(8,128)(2,1)}), bf16[128,6,1,1024]{3,1,2,0:T(8,128)(2,1)S(1)}, u32[]{:S(2)}, u32[]{:S(2)}) async-start(bf16[128,6,1,1024]{3,1,2,0:T(8,128)(2,1)} %bitcast.4), calls=%async_computation | async-start | bytes 4194304 | tf_op jit(solution)/shard_map/all_to_all | solution.py:32
  60.6 1.0 fusion.22
  61.6 2.1 fusion.11
  63.8 93.6 %all-to-all-done = bf16[128,6,1,1024]{3,1,2,0:T(8,128)(2,1)S(1)} async-done(((bf16[128,6,1,1024]{3,1,2,0:T(8,128)(2,1)}), bf16[128,6,1,1024]{3,1,2,0:T(8,128)(2,1)S(1)}, u32[]{:S(2)}, u32[]{:S(2)}) %all-to-all-start) | async-done | bytes 1572896 | tf_op jit(solution)/shard_map/all_to_all | solution.py:32
  157.3 4.1 %fusion.4 = f32[6,128,128]{2,1,0:T(8,128)} fusion(bf16[128,6,1,1024]{3,1,2,0:T(8,128)(2,1)S(1)} %all-to-all-done, bf16[6,128,1024]{2,0,1:T(8,128)(2,1)} %fusion.11), kind=kOutput, calls=%fused_computation.9 | convolution fusion | flops 201326592 | bytes 3538944 | tf_op jit(solution)/shard_map/sqf,spf->sqp/dot_general | solution.py:46
  161.8 52.1 %all-reduce.4.cloned.1.call-done = (f32[256,256]{1,0:T(8,128)}, f32[6,128,128]{2,1,0:T(8,128)}) async-done(((f32[256,256]{1,0:T(8,128)}, f32[6,128,128]{2,1,0:T(8,128)}), (f32[256,256]{1,0:T(8,128)}, f32[6,128,128]{2,1,0:T(8,128)})) %all-reduce.4.cloned.1.call-update) | async-done | bytes 655376 | tf_op jit(solution)/shard_map/psum | solution.py:47
  213.9 1.1 multiply_reduce_fusion.1
  215.0 1.2 multiply_reduce_fusion
  216.4 1.3 exponential_reduce_fusion
  217.8 1.8 select_reduce_fusion
  219.7 3.9 %fusion.6 = bf16[1,6,128,1024]{3,2,1,0:T(8,128)(2,1)S(1)} fusion(bf16[6,128,1024]{2,0,1:T(8,128)(2,1)} %fusion.11, f32[6,128,128]{2,1,0:T(8,128)} %get-tuple-element.8, f32[6,128]{1,0:T(8,128)S(1)} %get-tuple-element.6, f32[6,128]{1,0:T(8,128)S(1)} %get-tuple-element.5, pred[6]{0:T(512)(128)(4,1)S(1)} %lt.37), kind=kOutput, calls=%fused_computation.11 | convolution fusion | flops 203390976 | bytes 3545094 | tf_op jit(solution)/shard_map/sqp,sqf->spf/dot_general | solution.py:87
  223.6 2.2 copy.57
  225.9 19.0 %all-to-all-start.1 = ((bf16[1,6,128,1024]{3,1,0,2:T(8,128)(2,1)}), bf16[1,6,128,1024]{3,1,0,2:T(8,128)(2,1)}, u32[]{:S(2)}, u32[]{:S(2)}) async-start(bf16[1,6,128,1024]{3,1,0,2:T(8,128)(2,1)} %copy.57), calls=%async_computation.1 | async-start | bytes 4194304 | tf_op jit(solution)/shard_map/all_to_all | solution.py:89
  244.9 2.7 fusion.2
  247.6 3.7 %fusion = f32[2,128,1024]{2,0,1:T(2,128)S(1)} fusion(f32[6,128,1024]{2,1,0:T(8,128)S(1)} %fusion.2, s32[6]{0:T(128)S(1)} %copy-done.13), kind=kOutput, calls=%fused_computation.3 | convolution fusion | flops 18874380 | bytes 4194328 | tf_op jit(solution)/shard_map/sb,sqf->bqf/dot_general | solution.py:81
  253.1 1.2 fusion.8
  254.3 87.1 %all-to-all-done.1 = bf16[1,6,128,1024]{3,1,0,2:T(8,128)(2,1)} async-done(((bf16[1,6,128,1024]{3,1,0,2:T(8,128)(2,1)}), bf16[1,6,128,1024]{3,1,0,2:T(8,128)(2,1)}, u32[]{:S(2)}, u32[]{:S(2)}) %all-to-all-start.1) | async-done | bytes 1572896 | tf_op jit(solution)/shard_map/all_to_all | solution.py:89
  341.4 4.0 %convert_bitcast_fusion = f32[128,1,6,1,1024]{4,2,0,3,1:T(8,128)} fusion(bf16[1,6,128,1024]{3,1,0,2:T(8,128)(2,1)} %all-to-all-done.1), kind=kLoop, calls=%fused_computation.2 | loop fusion | flops 786432 | bytes 4718592 | tf_op jit(solution)/shard_map/convert_element_type | solution.py:102
  345.4 4.8 %reshape.221 = f32[768,1024]{1,0:T(8,128)} reshape(f32[128,1,6,1,1024]{4,2,0,3,1:T(8,128)} %convert_bitcast_fusion) | data formatting | bytes 6291456 | tf_op jit(solution)/shard_map/convert_element_type | solution.py:102
  350.2 10.9 %scatter_fusion = f32[256,1024]{1,0:T(8,128)S(1)} fusion(f32[256,1024]{1,0:T(8,128)S(1)} %convolution_multiply_fusion, s32[768]{0:T(1024)S(1)} %compare_select_fusion, f32[768,1024]{1,0:T(8,128)} %reshape.221), kind=kCustom, calls=%fused_computation.1 | custom fusion | flops 786432 | bytes 9440256 | tf_op jit(solution)/shard_map/scatter-add | solution.py:102
  (62 shorter events, 4.6 us)
Async XLA Ops:
  7.2 53.4 %copy-start = (bf16[256,1024]{1,0:T(8,128)(2,1)S(1)}, bf16[256,1024]{1,0:T(8,128)(2,1)}, u32[]{:S(2)}) copy-start(bf16[256,1024]{1,0:T(8,128)(2,1)} %param.6) | copy-start | bytes 1572868
  47.0 13.6 %copy-start.1 = (bf16[256,1,1024]{2,0,1:T(8,128)(2,1)S(1)}, bf16[256,1,1024]{2,0,1:T(8,128)(2,1)}, u32[]{:S(2)}) copy-start(bf16[256,1,1024]{2,0,1:T(8,128)(2,1)} %param.7) | copy-start | bytes 1572868
  47.0 110.3 %all-to-all-start = ((bf16[128,6,1,1024]{3,1,2,0:T(8,128)(2,1)}), bf16[128,6,1,1024]{3,1,2,0:T(8,128)(2,1)S(1)}, u32[]{:S(2)}, u32[]{:S(2)}) async-start(bf16[128,6,1,1024]{3,1,2,0:T(8,128)(2,1)} %bitcast.4), calls=%async_computation | async-start | bytes 4194304 | tf_op jit(solution)/shard_map/all_to_all | solution.py:32
  60.5 153.5 %all-reduce.4.cloned.1.call-start = ((), (), s32[]{:S(2)}) async-start(), calls=%async_computation.2 | async-start | bytes 1310720 | tf_op jit(solution)/shard_map/psum | solution.py:47
  60.6 101.0 %copy-start.12 = (s32[6]{0:T(128)}, s32[6]{0:T(128)S(1)}, u32[]{:S(2)}) copy-start(s32[6]{0:T(128)S(1)} %eq.77) | copy-start | bytes 76
  63.8 97.7 %copy-start.17 = (s32[2]{0:T(128)S(1)}, s32[2]{0:T(128)}, u32[]{:S(2)}) copy-start(s32[2]{0:T(128)} %param.9) | copy-start | bytes 28
  63.8 98.1 %copy-start.16 = (s32[256]{0:T(256)S(1)}, s32[256]{0:T(256)}, u32[]{:S(2)}) copy-start(s32[256]{0:T(256)} %param.10) | copy-start | bytes 3076
  63.8 155.8 %copy-start.4 = (f32[256]{0:T(256)S(1)}, f32[256]{0:T(256)}, u32[]{:S(2)}) copy-start(f32[256]{0:T(256)} %param.11) | copy-start | bytes 3076
  161.6 62.0 %copy-start.14 = (pred[6]{0:T(512)(128)(4,1)}, pred[6]{0:T(512)(128)(4,1)S(1)}, u32[]{:S(2)}) copy-start(pred[6]{0:T(512)(128)(4,1)S(1)} %lt.37) | copy-start | bytes 22
  216.2 7.4 %copy-start.6 = (f32[256]{0:T(256)}, f32[256]{0:T(256)S(1)}, u32[]{:S(2)}) copy-start(f32[256]{0:T(256)S(1)} %bitcast_maximum_fusion.1) | copy-start | bytes 3076
  217.8 1.9 copy-start.10
  219.5 4.1 %copy-start.8 = (f32[256]{0:T(256)}, f32[256]{0:T(256)S(1)}, u32[]{:S(2)}) copy-start(f32[256]{0:T(256)S(1)} %get-tuple-element.4) | copy-start | bytes 3076
  225.9 19.0 %copy-start.2 = (f32[6,128,128]{2,1,0:T(8,128)S(1)}, f32[6,128,128]{2,1,0:T(8,128)}, u32[]{:S(2)}) copy-start(f32[6,128,128]{2,1,0:T(8,128)} %get-tuple-element.8) | copy-start | bytes 1179652
  225.9 115.5 %all-to-all-start.1 = ((bf16[1,6,128,1024]{3,1,0,2:T(8,128)(2,1)}), bf16[1,6,128,1024]{3,1,0,2:T(8,128)(2,1)}, u32[]{:S(2)}, u32[]{:S(2)}) async-start(bf16[1,6,128,1024]{3,1,0,2:T(8,128)(2,1)} %copy.57), calls=%async_computation.1 | async-start | bytes 4194304 | tf_op jit(solution)/shard_map/all_to_all | solution.py:89
  244.9 2.7 copy-start.13
  251.3 0.7 copy-start.7
  251.3 0.7 copy-start.9
  251.4 0.7 copy-start.11
  251.4 0.7 copy-start.15
  251.4 1.2 copy-start.3
  251.4 1.2 copy-start.5
Sparse Core Ops, SparseCore 0:
  161.6 52.3 all-reduce.3
where the time goes:
time: 371 us; the launch traced here: 369 us
  waiting for transfers between devices  233 us (63%)
  starting transfers between devices  32.5 us (9%)
  blocking collectives  30.3 us (8%)
  other arithmetic  22.2 us (6%)
  matrix products  19.2 us (5%)
  local copies, waits for them, and re-layouts  16.9 us (5%)
  between operations  15 us (4%)
    all_to_all x1, waiting for transfers between devices, per_device(): lax.all_to_all(outgoing, 'dp', split_axis=0, concat_axis=2, tiled=True)  93.6 us
    all_to_all x1, waiting for transfers between devices, per_device(): lax.all_to_all(shares.reshape(1, slot_count, block_size, feature_width),...  87.1 us
    psum x1, waiting for transfers between devices, per_device(): full_in, full_list = lax.psum((part_in, part_list), 'grp')  52.1 us
    unnamed x1, blocking collectives  30.3 us
    all_to_all x1, starting transfers between devices, per_device(): lax.all_to_all(shares.reshape(1, slot_count, block_size, feature_width),...  19 us
    all_to_all x1, starting transfers between devices, per_device(): lax.all_to_all(outgoing, 'dp', split_axis=0, concat_axis=2, tiled=True)  13.5 us
    scatter-add x1, other arithmetic, per_device(): summed = own_part.reshape(block_total, shard_rows, feature_width).at[all_...  10.9 us
  transfers between devices with their start and end apart: 3, of which 3 were waited for; matrix products, arithmetic and copies ran while one was open for 3% of the time, Pallas kernels for 0%

commit v1 on v0

v1 whole, which is shorter than its diff:
```python
import functools
import math

import jax
import jax.numpy as jnp
from jax import lax
from jax.experimental import pallas as pl
from jax.experimental.pallas import tpu as pltpu
from jax.sharding import PartitionSpec as P

D = 4096
SCALE = 3.0 / math.sqrt(D)
SLOTS = 4
LOGICAL = pl.DeviceIdType.LOGICAL
NN = (((1,), (0,)), ((), ()))
NT = (((1,), (1,)), ((), ()))
F32, BF16 = jnp.float32, jnp.bfloat16


def mm(a, b, dims=NN):
    return lax.dot_general(a, b, dims, preferred_element_type=F32)


def kernel(
    z_count,
    q_ref, p_ref, lists_ref, lens_ref, pos_ref, lg_ref,
    loss_ref, gq_ref, gp_ref,
    ids, send1, recv1, send2, recv2, wide, listed, hot_t,
    part_in, recv_in, part_l, recv_l, sum_in, cols,
    wl_all, wi_all, ls_all, w_in, w_full, w_full_t, own,
    ids_s, ids_r, e1_s, e1_r, e2_s, e2_r, ri_s, ri_r, rl_s, rl_r, al_s, al_r, ai_s, ai_r, ls_s, ls_r, loc,
):
    me = lax.axis_index("dp")
    y = lax.axis_index("grp")
    n_dp = lax.axis_size("dp")
    n_y = lax.axis_size("grp")
    plane = n_dp // z_count
    my_z, my_xc = me // plane, me % plane
    block = q_ref.shape[0] // 2
    rows = block // n_y
    chunks = q_ref.shape[1] // 128
    msg = SLOTS * chunks

    def device(p, g):
        return p * n_y + g

    def copy_to(src, dst, ss, rs, dev):
        return pltpu.make_async_remote_copy(
            src_ref=src, dst_ref=dst, send_sem=ss, recv_sem=rs, device_id=dev, device_id_type=LOGICAL
        )

    def wait_bytes(ref, sem):
        pltpu.make_async_copy(ref, ref, sem).wait()

    def each_peer(body):
        def step(p, carry):
            body(p)
            return carry

        lax.fori_loop(me + 1, n_dp, step, 0)
        lax.fori_loop(0, me, step, 0)

    def far_first(body):
        def step(i, carry):
            j = z_count - 1 - i // plane
            k = plane - 1 - i % plane
            half = (j + 1) // 2
            dz = jnp.where(j % 2 == 1, half, z_count - half)
            body((my_z + dz) % z_count * plane + (my_xc + k) % plane)
            return carry

        lax.fori_loop(0, n_dp - 1, step, 0)

    barrier = pltpu.get_barrier_semaphore()
    each_peer(
        lambda p: pl.semaphore_signal(barrier, inc=1, device_id=device(p, y), device_id_type=LOGICAL)
    )
    for k in range(1, n_y):
        pl.semaphore_signal(
            barrier, inc=1, device_id=device(me, (y + k) % n_y), device_id_type=LOGICAL
        )

    len0, len1 = lens_ref[0], lens_ref[1]
    lane = lax.broadcasted_iota(jnp.int32, (1, 128), 1)
    id_row = jnp.full((1, 128), -1, jnp.int32)
    owner = []
    for s in range(SLOTS):
        k = s - len0
        second = jnp.where(
            k == 0, lists_ref[1, 0], jnp.where(k == 1, lists_ref[1, 1], lists_ref[1, 2])
        )
        first = lists_ref[0, min(s, 2)]
        in0 = jnp.int32(s) < len0
        in1 = k < len1
        slot_id = jnp.where(in0, first, jnp.where(in1, second, -1))
        owner.append(jnp.where(in0, 0, jnp.where(in1, 1, 2)))
        id_row = jnp.where(lane == s, slot_id, id_row)
    ids[me] = id_row

    scores = mm(q_ref[...], p_ref[...], NT)
    for g in range(n_y):
        for b in range(2):
            part_in[g, b * rows : (b + 1) * rows, :] = scores[
                b * block + g * rows : b * block + (g + 1) * rows
            ]
    for b in range(2):
        cols[0, b * block : (b + 1) * block, :] = jnp.broadcast_to(
            lg_ref[b : b + 1, :], (block, 128)
        ).T
        column = (pos_ref[b : b + 1, :] // block).astype(F32)
        cols[1, b * block : (b + 1) * block, :] = jnp.broadcast_to(column, (block, 128)).T

    pl.semaphore_wait(barrier, n_dp - 1 + n_y - 1)

    each_peer(lambda p: copy_to(ids.at[me], ids.at[me], ids_s, ids_r, device(p, y)).start())
    for k in range(1, n_y):
        g = (y + k) % n_y
        copy_to(part_in.at[g], recv_in.at[y], ri_s, ri_r, device(me, g)).start()
    wait_bytes(ids.at[pl.ds(0, n_dp - 1)], ids_r)

    id_mat = ids[...].reshape(n_dp, 128)
    number = lax.broadcasted_iota(jnp.int32, (n_dp, p_ref.shape[0]), 1)
    hots = [(id_mat[:, s : s + 1] == number).astype(F32) for s in range(SLOTS)]

    def to_messages(value, s, c):
        for h in range(2):
            wide[pl.ds(s * chunks + 2 * c + h, n_dp, stride=msg), :] = value[
                :, h * 128 : (h + 1) * 128
            ]

    def from_messages():
        for s in range(SLOTS):
            for c in range(chunks):
                listed[s * n_dp : (s + 1) * n_dp, c * 128 : (c + 1) * 128] = wide[
                    pl.ds(s * chunks + c, n_dp, stride=msg), :
                ].astype(BF16)

    step_rows = 512

    def narrow(dst):
        def step(i, carry):
            at = pl.ds(pl.multiple_of(i * step_rows, step_rows), step_rows)
            dst[at, :] = wide[at, :].astype(BF16)
            return carry

        lax.fori_loop(0, n_dp * msg // step_rows, step, 0)

    def widen(src):
        def step(i, carry):
            at = pl.ds(pl.multiple_of(i * step_rows, step_rows), step_rows)
            wide[at, :] = src[at, :].astype(F32)
            return carry

        lax.fori_loop(0, n_dp * msg // step_rows, step, 0)

    for s in range(SLOTS):
        hot = hots[s].astype(BF16)
        for c in range(chunks // 2):
            to_messages(mm(hot, p_ref[:, c * 256 : (c + 1) * 256]), s, c)
    narrow(send1)

    def at_row(ref, p):
        return ref.at[pl.ds(pl.multiple_of(p * msg, msg), msg)]

    def exchange(src, dst, ss, rs):
        far_first(
            lambda p: copy_to(at_row(src, p), at_row(dst, me), ss, rs, device(p, y)).start()
        )
        pltpu.make_async_copy(at_row(src, me), at_row(dst, me), loc).start()

    def finish(dst, rs):
        wait_bytes(dst.at[pl.ds(0, (n_dp - 1) * msg)], rs)
        wait_bytes(at_row(dst, me), loc)

    exchange(send1, recv1, e1_s, e1_r)

    for s in range(SLOTS):
        hot_t[:, s * n_dp : (s + 1) * n_dp] = hots[s].T.astype(BF16)
    recv_in[y] = part_in[y]
    wait_bytes(recv_in.at[pl.ds(0, n_y - 1)], ri_r)
    total = recv_in[0]
    for g in range(1, n_y):
        total = total + recv_in[g]
    sum_in[...] = SCALE * total

    finish(recv1, e1_r)
    widen(recv1)
    from_messages()
    scores_l = mm(q_ref[...], listed[...], NT)
    for s in range(SLOTS):
        mine = jnp.where(
            jnp.full((block, 128), owner[s]) == 1,
            scores_l[block:, s * n_dp : (s + 1) * n_dp],
            scores_l[:block, s * n_dp : (s + 1) * n_dp],
        )
        for g in range(n_y):
            part_l[g, s] = mine[g * rows : (g + 1) * rows]
    for k in range(1, n_y):
        g = (y + k) % n_y
        copy_to(part_l.at[g], recv_l.at[y], rl_s, rl_r, device(me, g)).start()
    recv_l[y] = part_l[y]

    own_cols = []
    for b in range(2):
        at = pl.ds(pl.multiple_of(b * block + y * rows, rows), rows)
        own_cols.append((cols[0, at, :][:, :1], cols[1, at, :][:, :1]))
    wait_bytes(recv_l.at[pl.ds(0, n_y - 1)], rl_r)
    slot_scores = []
    for s in range(SLOTS):
        t = recv_l[0, s]
        for g in range(1, n_y):
            t = t + recv_l[g, s]
        slot_scores.append(SCALE * t)
    logs = []
    for b in range(2):
        sc = sum_in[b * rows : (b + 1) * rows, :]
        opened = [
            jnp.where(jnp.full((rows, 128), owner[s]) == b, slot_scores[s], -jnp.inf)
            for s in range(SLOTS)
        ]
        top = jnp.max(sc, axis=1, keepdims=True)
        for o in opened:
            top = jnp.maximum(top, jnp.max(o, axis=1, keepdims=True))
        acc = jnp.sum(jnp.exp(sc - top), axis=1, keepdims=True)
        for o in opened:
            acc = acc + jnp.sum(jnp.exp(o - top), axis=1, keepdims=True)
        logs.append(top + jnp.log(acc))
    for s in range(SLOTS):
        which = jnp.full((rows, 1), owner[s])
        log_s = jnp.where(which == 1, logs[1], logs[0])
        grad_s = jnp.where(which == 1, own_cols[1][0], own_cols[0][0])
        weight = grad_s * jnp.exp(slot_scores[s] - log_s)
        weight = jnp.where(jnp.full((rows, 128), owner[s]) == 2, 0.0, weight)
        wl_all[y, s] = weight.astype(BF16)
    for k in range(1, n_y):
        g = (y + k) % n_y
        copy_to(wl_all.at[y], wl_all.at[y], al_s, al_r, device(me, g)).start()

    number_in = lax.broadcasted_iota(jnp.int32, (rows, p_ref.shape[0]), 1).astype(F32)
    ls_all[y] = jnp.zeros((8, 128), F32)
    for b in range(2):
        sc = sum_in[b * rows : (b + 1) * rows, :]
        positive = number_in == own_cols[b][1]
        loss = logs[b] - jnp.sum(jnp.where(positive, sc, 0.0), axis=1, keepdims=True)
        weight = own_cols[b][0] * (jnp.exp(sc - logs[b]) - positive.astype(F32))
        wi_all[y, b * rows : (b + 1) * rows, :] = weight.astype(BF16)
        place = lax.broadcasted_iota(jnp.int32, (rows, 128), 1) - y * rows
        diag = place == lax.broadcasted_iota(jnp.int32, (rows, 128), 0)
        ls_all[y, b : b + 1, :] = jnp.sum(jnp.where(diag, loss, 0.0), axis=0, keepdims=True)

    wait_bytes(wl_all.at[pl.ds(0, n_y - 1)], al_r)
    for s in range(SLOTS):
        w_s = jnp.concatenate([wl_all[g, s].astype(F32) for g in range(n_y)], axis=0)
        w_t = w_s.T
        for b in range(2):
            keep = jnp.where(jnp.full((block, 128), owner[s]) == b, 1.0, 0.0)
            w_full[b * block : (b + 1) * block, s * 128 : (s + 1) * 128] = (w_s * keep).astype(BF16)
            w_full_t[s * 128 : (s + 1) * 128, b * block : (b + 1) * block] = (w_t * keep).astype(BF16)
    for s in range(SLOTS):
        for c in range(chunks // 2):
            share = mm(
                w_full_t[s * 128 : (s + 1) * 128, :], q_ref[:, c * 256 : (c + 1) * 256]
            )
            to_messages(SCALE * share, s, c)
    narrow(send2)
    exchange(send2, recv2, e2_s, e2_r)

    for k in range(1, n_y):
        g = (y + k) % n_y
        copy_to(wi_all.at[y], wi_all.at[y], ai_s, ai_r, device(me, g)).start()
        copy_to(ls_all.at[y], ls_all.at[y], ls_s, ls_r, device(me, g)).start()
    wait_bytes(wi_all.at[pl.ds(0, n_y - 1)], ai_r)
    wait_bytes(ls_all.at[pl.ds(0, n_y - 1)], ls_r)
    loss_all = ls_all[0]
    for g in range(1, n_y):
        loss_all = loss_all + ls_all[g]
    loss_ref[...] = loss_all[0:2, :]
    for b in range(2):
        for g in range(n_y):
            w_in[b * block + g * rows : b * block + (g + 1) * rows, :] = wi_all[
                g, b * rows : (b + 1) * rows, :
            ]
    w_in_t = w_in[...].astype(F32).T.astype(BF16)
    for c in range(chunks // 2):
        cc = slice(c * 256, (c + 1) * 256)
        grad = mm(w_in[...], p_ref[:, cc]) + mm(w_full[...], listed[:, cc])
        gq_ref[:, cc] = (SCALE * grad).astype(BF16)
        own[:, cc] = SCALE * mm(w_in_t, q_ref[:, cc])

    finish(recv2, e2_r)
    widen(recv2)
    from_messages()
    for c in range(chunks // 2):
        cc = slice(c * 256, (c + 1) * 256)
        gp_ref[:, cc] = (own[:, cc] + mm(hot_t[...], listed[:, cc])).astype(BF16)

    wait_bytes(ids.at[pl.ds(0, n_dp - 1)], ids_s)
    wait_bytes(recv1.at[pl.ds(0, (n_dp - 1) * msg)], e1_s)
    wait_bytes(recv1.at[pl.ds(0, (n_dp - 1) * msg)], e2_s)
    wait_bytes(recv_in.at[pl.ds(0, n_y - 1)], ri_s)
    wait_bytes(recv_l.at[pl.ds(0, n_y - 1)], rl_s)
    wait_bytes(wl_all.at[pl.ds(0, n_y - 1)], al_s)
    wait_bytes(wi_all.at[pl.ds(0, n_y - 1)], ai_s)
    wait_bytes(ls_all.at[pl.ds(0, n_y - 1)], ls_s)


def per_device(z_count, queries, passages, block_lists, list_lengths, positive, loss_grad):
    n_dp, n_y = lax.axis_size("dp"), lax.axis_size("grp")
    n_blocks, shard_rows, width = passages.shape
    n_q = queries.shape[0]
    block = n_q // 2
    rows = block // n_y
    chunks = width // 128
    msg = SLOTS * chunks
    vmem = pl.BlockSpec(memory_space=pltpu.VMEM)
    smem = pl.BlockSpec(memory_space=pltpu.SMEM)
    big = (n_dp * msg, 128)
    losses, gq, gp = pl.pallas_call(
        functools.partial(kernel, z_count),
        out_shape=(
            jax.ShapeDtypeStruct((2, block), F32),
            jax.ShapeDtypeStruct((n_q, width), BF16),
            jax.ShapeDtypeStruct((n_blocks, width), BF16),
        ),
        in_specs=[vmem, vmem, smem, smem, vmem, vmem],
        out_specs=(vmem, vmem, vmem),
        scratch_shapes=[
            pltpu.VMEM((n_dp, 1, 128), jnp.int32),
            pltpu.VMEM(big, BF16),
            pltpu.VMEM(big, BF16),
            pltpu.VMEM(big, BF16),
            pltpu.VMEM(big, BF16),
            pltpu.VMEM(big, F32),
            pltpu.VMEM((SLOTS * n_dp, width), BF16),
            pltpu.VMEM((n_blocks, SLOTS * n_dp), BF16),
            pltpu.VMEM((n_y, 2 * rows, n_blocks), F32),
            pltpu.VMEM((n_y, 2 * rows, n_blocks), F32),
            pltpu.VMEM((n_y, SLOTS, rows, 128), F32),
            pltpu.VMEM((n_y, SLOTS, rows, 128), F32),
            pltpu.VMEM((2 * rows, n_blocks), F32),
            pltpu.VMEM((2, n_q, 128), F32),
            pltpu.VMEM((n_y, SLOTS, rows, 128), BF16),
            pltpu.VMEM((n_y, 2 * rows, n_blocks), BF16),
            pltpu.VMEM((n_y, 8, 128), F32),
            pltpu.VMEM((n_q, n_blocks), BF16),
            pltpu.VMEM((n_q, SLOTS * 128), BF16),
            pltpu.VMEM((SLOTS * 128, n_q), BF16),
            pltpu.VMEM((n_blocks, width), F32),
        ]
        + [pltpu.SemaphoreType.DMA] * 17,
        name="loss_and_gradients",
        compiler_params=pltpu.CompilerParams(
            collective_id=0, has_side_effects=True, vmem_limit_bytes=40 * 2**20
        ),
    )(
        queries,
        passages.reshape(n_blocks * shard_rows, width),
        block_lists,
        list_lengths,
        positive.reshape(2, block),
        loss_grad.reshape(2, block),
    )
    return losses.reshape(n_q), gq, gp.reshape(passages.shape)


def solution(mesh):
    in_specs = (P("dp", "grp"), P(None, "dp", "grp"), P("dp", None), P("dp"), P("dp"), P("dp"))
    out_specs = (P("dp"), P("dp", "grp"), P(None, "dp", "grp"))
    z_count = mesh.shape["dp"] // 8
    return jax.shard_map(
        functools.partial(per_device, z_count),
        mesh=mesh, in_specs=in_specs, out_specs=out_specs, check_vma=False,
    )
```

time: 371 us -> 146 us (0.39)
  waiting for transfers between devices: 233 us -> 0 us
  Pallas kernels: 0 us -> 140 us
  starting transfers between devices: 32.5 us -> 0 us
  blocking collectives: 30.3 us -> 0 us
  other arithmetic: 22.2 us -> 0 us
  matrix products: 19.2 us -> 0 us
  between operations: 15 us -> 0.68 us
  local copies, waits for them, and re-layouts: 16.9 us -> 4.91 us
    all_to_all x2 -> x0, waiting for transfers between devices: 181 us -> none  [the longest x1 93.6 us: per_device(): lax.all_to_all(outgoing, 'dp', split_axis=0, concat_axis=2, tiled=True)]
    pallas_call x0 -> x1, Pallas kernels: none -> 140 us  [per_device(): pl.pallas_call(functools.partial(kernel, z_count), out_shape=(jax.ShapeDt...]
    psum x1 -> x0, waiting for transfers between devices: 52.1 us -> none  [per_device(): full_in, full_list = lax.psum((part_in, part_list), 'grp')]
    all_to_all x2 -> x0, starting transfers between devices: 32.5 us -> none  [the longest x1 19 us: per_device(): lax.all_to_all(shares.reshape(1, slot_count, block_size, feature_width),...]
    unnamed x1 -> x0, blocking collectives: 30.3 us -> none
    dot_general x8 -> x0, matrix products: 19.2 us -> none  [the longest x1 4.09 us: per_device(): jnp.einsum('sqf,spf->sqp', chosen, fetched, preferred_element_type=jnp.fl...]
    scatter-add x1 -> x0, other arithmetic: 10.9 us -> none  [per_device(): summed = own_part.reshape(block_total, shard_rows, feature_width).at[all_...]
    gather x1 -> x0, local copies, waits for them, and re-layouts: 4.93 us -> none  [per_device(): passages[all_ids].reshape(dp_count, slot_count, shard_rows, feature_width)]
  transfers between devices with their start and end apart: 3 -> 0, of which waited for: 3 -> 0; matrix products, arithmetic and copies ran while one was open for 3% -> 0% of each run, Pallas kernels for 0% -> 0%
where the time goes in v1:
time: 146 us
  Pallas kernels  140 us (96%)
  local copies, waits for them, and re-layouts  4.91 us (3%)
    pallas_call x1, Pallas kernels, per_device(): pl.pallas_call(functools.partial(kernel, z_count), out_shape=(jax.ShapeDt...  140 us
    unnamed x15, local copies, waits for them, and re-layouts  4.91 us

profile of v1, /device:TPU:1, one launch (start us, length us, event | category | flops | bytes accessed | tf_op | source)
XLA Modules:
  0.0 145.7 jit_solution(416738591611423021)
XLA Ops:
  0.6 0.0 copy-start.3
  0.6 0.0 copy-start.4
  0.7 0.0 copy-start.2
  0.7 0.0 copy-start.5
  0.7 0.6 copy-done.3
  1.3 0.0 copy-done.4
  1.3 0.0 copy-done.2
  1.3 0.0 copy-done.5
  1.3 0.0 copy-start
  1.3 1.0 copy-done
  2.4 0.0 copy-start.1
  2.4 1.0 copy-done.1
  3.4 140.1 %loss_and_gradients.1 = (f32[2,128]{1,0:T(2,128)S(1)}, bf16[256,1024]{1,0:T(8,128)(2,1)S(1)}, bf16[256,1024]{1,0:T(8,128)(2,1)S(1)}) custom-call(bf16[256,1024]{1,0:T(8,128)(2,1)S(1)} %copy-done, bf16[256,1024]{1,0:T(8,128)(2,1)S(1)} %bitcast.5, s32[2,3]{1,0:T(2,128)S(1)} %copy-done.2, s32[2]{0:T(128)S(1)} %copy-done.5, s32[2,128]{1,0:T(2,128)S(1)} %bitcast.7, ...), custom_call_target="tpu_custom_call" | custom-call | tf_op jit(solution)/shard_map/loss_and_gradients/pallas_call | solution.py:318
  143.6 0.6 copy.12
  144.1 0.8 copy.13
  144.9 0.8 copy.14
Async XLA Ops:
  0.6 0.7 copy-start.3
  0.6 0.7 copy-start.4
  0.7 0.7 copy-start.2
  0.7 0.7 copy-start.5
  1.3 1.0 copy-start
  2.4 1.0 copy-start.1

commit v2 on v1

v2 whole, which is shorter than its diff:
```python
import functools
import math

import jax
import jax.numpy as jnp
from jax import lax
from jax.experimental import pallas as pl
from jax.experimental.pallas import tpu as pltpu
from jax.sharding import PartitionSpec as P

D = 4096
SCALE = 3.0 / math.sqrt(D)
SLOTS = 4
LOGICAL = pl.DeviceIdType.LOGICAL
NN = (((1,), (0,)), ((), ()))
NT = (((1,), (1,)), ((), ()))
F32, BF16 = jnp.float32, jnp.bfloat16


def mm(a, b, dims=NN):
    return lax.dot_general(a, b, dims, preferred_element_type=F32)


def kernel(
    z_count,
    q_hbm, p_hbm, lists_hbm, lens_hbm, pos_hbm, lg_hbm,
    loss_ref, gq_ref, gp_ref,
    q_ref, p_ref, lists_ref, lens_ref, pos_ref, lg_ref,
    ids, send1, recv1, send2, recv2, wide, listed, shared, hot_t,
    part_in, recv_in, part_l, recv_l, sum_in, sum_l, cols,
    wl_all, wi_all, ls_all, w_in, w_full, w_full_t, own,
    in_s, loc, sent, ids_r, e1_r, e2_r, ri_r, rl_r, al_r, ai_r, ls_r,
):
    me = lax.axis_index("dp")
    y = lax.axis_index("grp")
    n_dp = lax.axis_size("dp")
    n_y = lax.axis_size("grp")
    plane = n_dp // z_count
    my_z, my_xc = me // plane, me % plane
    block = q_ref.shape[0] // 2
    rows = block // n_y
    chunks = q_ref.shape[1] // 128
    msg = SLOTS * chunks
    far = z_count // 2
    order = [far, far - 1, 1 - far, 0]
    for h in range(far - 2, 0, -1):
        order += [h, -h]
    opposite = [order.index(-dz) if -dz in order else order.index(dz) for dz in order]
    parts = z_count // 4
    peers = 4 * plane
    part_rows = peers * msg
    lanes = SLOTS * peers
    zs = [lax.rem(my_z + dz + z_count, z_count) for dz in order]
    base = [z * (plane * n_y) + y for z in zs]

    def copy_to(src, dst, ss, rs, dev):
        return pltpu.make_async_remote_copy(
            src_ref=src, dst_ref=dst, send_sem=ss, recv_sem=rs, device_id=dev, device_id_type=LOGICAL
        )

    def wait_bytes(ref, sem):
        pltpu.make_async_copy(ref, ref, sem).wait()

    def y_peers(body):
        for k in range(1, n_y):
            g = lax.rem(y + k, n_y)
            body(g, me * n_y + g)

    def part_peers(t, body):
        def step(k, carry):
            xc = lax.rem(my_xc + k, plane)
            for i in range(4 * t, 4 * t + 4):
                body(i * plane + xc, opposite[i] * plane + my_xc, base[i] + xc * n_y)
            return carry

        lax.fori_loop(1, plane, step, 0)
        for i in range(4 * t, 4 * t + 4):
            if order[i] != 0:
                body(i * plane + my_xc, opposite[i] * plane + my_xc, base[i] + my_xc * n_y)

    my_place = order.index(0) * plane + my_xc
    copies_in = [
        pltpu.make_async_copy(src, dst, in_s.at[k])
        for k, (src, dst) in enumerate(
            (
                (lists_hbm, lists_ref), (lens_hbm, lens_ref), (q_hbm, q_ref),
                (p_hbm, p_ref), (pos_hbm, pos_ref), (lg_hbm, lg_ref),
            )
        )
    ]
    for c in copies_in:
        c.start()

    barrier = pltpu.get_barrier_semaphore()

    def greet(dev):
        pl.semaphore_signal(barrier, inc=1, device_id=dev, device_id_type=LOGICAL)

    def greet_z(i, carry):
        z = lax.rem(my_z + i, z_count)
        for xc in range(plane):
            greet((z * plane + xc) * n_y + y)
        return carry

    lax.fori_loop(1, z_count, greet_z, 0)
    for k in range(1, plane):
        greet((my_z * plane + lax.rem(my_xc + k, plane)) * n_y + y)
    y_peers(lambda g, dev: greet(dev))

    copies_in[0].wait()
    copies_in[1].wait()
    len0, len1 = lens_ref[0], lens_ref[1]
    lane = lax.broadcasted_iota(jnp.int32, (1, 128), 1)
    id_row = jnp.full((1, 128), -1, jnp.int32)
    owner = jnp.full((1, lanes), 2, jnp.int32)
    slot_lane = lax.broadcasted_iota(jnp.int32, (1, lanes), 1) // peers
    for s in range(SLOTS):
        k = s - len0
        second = jnp.where(
            k == 0, lists_ref[1, 0], jnp.where(k == 1, lists_ref[1, 1], lists_ref[1, 2])
        )
        first = lists_ref[0, min(s, 2)]
        in0 = jnp.int32(s) < len0
        in1 = k < len1
        slot_id = jnp.where(in0, first, jnp.where(in1, second, -1))
        owner = jnp.where(slot_lane == s, jnp.where(in0, 0, jnp.where(in1, 1, 2)), owner)
        id_row = jnp.where(lane == s, slot_id, id_row)
    ids[my_place] = id_row

    for c in copies_in[2:]:
        c.wait()
    scores = mm(q_ref[...], p_ref[...], NT)
    for g in range(n_y):
        for b in range(2):
            part_in[g, b * rows : (b + 1) * rows, :] = scores[
                b * block + g * rows : b * block + (g + 1) * rows
            ]

    pl.semaphore_wait(barrier, n_dp - 1 + n_y - 1)

    for t in range(parts):
        part_peers(
            t,
            lambda i, there, dev: copy_to(
                ids.at[my_place], ids.at[there], sent.at[0], ids_r.at[t], dev
            ).start(),
        )

    def part_sizes(t):
        return peers - 1 if t == order.index(0) // 4 else peers

    def to_messages(value, t, c):
        for s in range(SLOTS):
            for h in range(2):
                wide[pl.ds(t * part_rows + s * chunks + 2 * c + h, peers, stride=msg), :] = value[
                    s * peers : (s + 1) * peers, h * 128 : (h + 1) * 128
                ]

    def narrow(dst, t):
        at = slice(t * part_rows, (t + 1) * part_rows)
        dst[at, :] = wide[at, :].astype(BF16)

    def from_messages(src, dst, t):
        at = slice(t * part_rows, (t + 1) * part_rows)
        wide[at, :] = src[at, :].astype(F32)
        for s in range(SLOTS):
            for c in range(chunks):
                dst[t * lanes + s * peers : t * lanes + (s + 1) * peers, c * 128 : (c + 1) * 128] = wide[
                    pl.ds(t * part_rows + s * chunks + c, peers, stride=msg), :
                ].astype(BF16)

    def at_row(ref, p):
        return ref.at[pl.ds(pl.multiple_of(p * msg, msg), msg)]

    def send_part(t, src, dst, ss, rs):
        part_peers(
            t,
            lambda i, there, dev: copy_to(
                at_row(src, i), at_row(dst, there), ss, rs.at[t], dev
            ).start(),
        )
        if t == order.index(0) // 4:
            pltpu.make_async_copy(at_row(src, my_place), at_row(dst, my_place), loc).start()

    def wait_part(t, dst, rs):
        wait_bytes(dst.at[pl.ds(t * part_rows, part_sizes(t) * msg)], rs.at[t])
        if t == order.index(0) // 4:
            wait_bytes(at_row(dst, my_place), loc)

    number = lax.broadcasted_iota(jnp.int32, (peers, p_ref.shape[0]), 1)
    for t in range(parts):
        wait_bytes(ids.at[pl.ds(t * peers, part_sizes(t))], ids_r.at[t])
        id_mat = ids[t * peers : (t + 1) * peers].reshape(peers, 128)
        hot = jnp.concatenate(
            [(id_mat[:, s : s + 1] == number).astype(F32) for s in range(SLOTS)], axis=0
        )
        hot_16 = hot.astype(BF16)
        for c in range(chunks // 2):
            to_messages(mm(hot_16, p_ref[:, c * 256 : (c + 1) * 256]), t, c)
        narrow(send1, t)
        send_part(t, send1, recv1, sent.at[1], e1_r)
        hot_t[:, t * lanes : (t + 1) * lanes] = hot.T.astype(BF16)

    y_peers(lambda g, dev: copy_to(part_in.at[g], recv_in.at[y], sent.at[2], ri_r, dev).start())
    for b in range(2):
        cols[0, b * block : (b + 1) * block, :] = jnp.broadcast_to(
            lg_ref[b : b + 1, :], (block, 128)
        ).T
        column = (pos_ref[b : b + 1, :] // block).astype(F32)
        cols[1, b * block : (b + 1) * block, :] = jnp.broadcast_to(column, (block, 128)).T
    recv_in[y] = part_in[y]
    wait_bytes(recv_in.at[pl.ds(0, n_y - 1)], ri_r)
    total = recv_in[0]
    for g in range(1, n_y):
        total = total + recv_in[g]
    sum_in[...] = SCALE * total

    def add_scores(t):
        wait_bytes(recv_l.at[t, pl.ds(0, n_y - 1)], rl_r.at[t])
        total = recv_l[t, 0]
        for g in range(1, n_y):
            total = total + recv_l[t, g]
        sum_l[t] = SCALE * total

    for t in range(parts):
        wait_part(t, recv1, e1_r)
        from_messages(recv1, listed, t)
        scores = mm(q_ref[...], listed[t * lanes : (t + 1) * lanes, :], NT)
        mine = jnp.where(jnp.broadcast_to(owner == 1, (block, lanes)), scores[block:], scores[:block])
        for g in range(n_y):
            part_l[t, g] = mine[g * rows : (g + 1) * rows]
        y_peers(
            lambda g, dev: copy_to(
                part_l.at[t, g], recv_l.at[t, y], sent.at[3], rl_r.at[t], dev
            ).start()
        )
        recv_l[t, y] = part_l[t, y]
        if t > 0:
            add_scores(t - 1)
    add_scores(parts - 1)

    own_cols = []
    for b in range(2):
        at = pl.ds(pl.multiple_of(b * block + y * rows, rows), rows)
        own_cols.append((cols[0, at, :][:, :1], cols[1, at, :][:, :1]))
    of_block = [jnp.broadcast_to(owner == b, (rows, lanes)) for b in range(2)]
    logs = []
    for b in range(2):
        sc = sum_in[b * rows : (b + 1) * rows, :]
        opened = [jnp.where(of_block[b], sum_l[t], -jnp.inf) for t in range(parts)]
        best = opened[0]
        for o in opened[1:]:
            best = jnp.maximum(best, o)
        top = jnp.maximum(
            jnp.max(sc, axis=1, keepdims=True), jnp.max(best, axis=1, keepdims=True)
        )
        terms = jnp.exp(opened[0] - top)
        for o in opened[1:]:
            terms = terms + jnp.exp(o - top)
        acc = jnp.sum(jnp.exp(sc - top), axis=1, keepdims=True) + jnp.sum(
            terms, axis=1, keepdims=True
        )
        logs.append(top + jnp.log(acc))
    log_l = jnp.where(of_block[1], logs[1], logs[0])
    grad_l = jnp.where(of_block[1], own_cols[1][0], own_cols[0][0])
    dead = jnp.broadcast_to(owner == 2, (rows, lanes))
    for t in range(parts):
        weight = jnp.where(dead, 0.0, grad_l * jnp.exp(sum_l[t] - log_l))
        wl_all[t, y] = weight.astype(BF16)
        y_peers(
            lambda g, dev: copy_to(
                wl_all.at[t, y], wl_all.at[t, y], sent.at[4], al_r.at[t], dev
            ).start()
        )

    number_in = lax.broadcasted_iota(jnp.int32, (rows, p_ref.shape[0]), 1).astype(F32)
    ls_all[y] = jnp.zeros((8, 128), F32)
    for b in range(2):
        sc = sum_in[b * rows : (b + 1) * rows, :]
        positive = number_in == own_cols[b][1]
        loss = logs[b] - jnp.sum(jnp.where(positive, sc, 0.0), axis=1, keepdims=True)
        weight = own_cols[b][0] * (jnp.exp(sc - logs[b]) - positive.astype(F32))
        wi_all[y, b * rows : (b + 1) * rows, :] = weight.astype(BF16)
        place = lax.broadcasted_iota(jnp.int32, (rows, 128), 1) - y * rows
        diag = place == lax.broadcasted_iota(jnp.int32, (rows, 128), 0)
        ls_all[y, b : b + 1, :] = jnp.sum(jnp.where(diag, loss, 0.0), axis=0, keepdims=True)

    for t in range(parts):
        wait_bytes(wl_all.at[t, pl.ds(0, n_y - 1)], al_r.at[t])
        w_t = jnp.concatenate([wl_all[t, g].astype(F32) for g in range(n_y)], axis=0)
        for b in range(2):
            w_b = jnp.where(jnp.broadcast_to(owner == b, (block, lanes)), w_t, 0.0)
            w_full[b * block : (b + 1) * block, t * lanes : (t + 1) * lanes] = w_b.astype(BF16)
            w_full_t[t * lanes : (t + 1) * lanes, b * block : (b + 1) * block] = w_b.T.astype(BF16)
        for c in range(chunks // 2):
            share = mm(
                w_full_t[t * lanes : (t + 1) * lanes, :], q_ref[:, c * 256 : (c + 1) * 256]
            )
            to_messages(SCALE * share, t, c)
        narrow(send2, t)
        send_part(t, send2, recv2, sent.at[5], e2_r)

    y_peers(lambda g, dev: copy_to(wi_all.at[y], wi_all.at[y], sent.at[6], ai_r, dev).start())
    y_peers(lambda g, dev: copy_to(ls_all.at[y], ls_all.at[y], sent.at[7], ls_r, dev).start())
    wait_bytes(wi_all.at[pl.ds(0, n_y - 1)], ai_r)
    wait_bytes(ls_all.at[pl.ds(0, n_y - 1)], ls_r)
    loss_all = ls_all[0]
    for g in range(1, n_y):
        loss_all = loss_all + ls_all[g]
    loss_ref[...] = loss_all[0:2, :]
    for b in range(2):
        for g in range(n_y):
            w_in[b * block + g * rows : b * block + (g + 1) * rows, :] = wi_all[
                g, b * rows : (b + 1) * rows, :
            ]
    w_in_t = w_in[...].astype(F32).T.astype(BF16)
    for c in range(chunks // 2):
        cc = slice(c * 256, (c + 1) * 256)
        grad = mm(w_in[...], p_ref[:, cc]) + mm(w_full[...], listed[:, cc])
        gq_ref[:, cc] = (SCALE * grad).astype(BF16)
        own[:, cc] = SCALE * mm(w_in_t, q_ref[:, cc])

    half = lanes * parts // 2
    for t in range(parts):
        wait_part(t, recv2, e2_r)
        from_messages(recv2, shared, t)
        if 2 * (t + 1) == parts:
            for c in range(chunks // 2):
                cc = slice(c * 256, (c + 1) * 256)
                own[:, cc] += mm(hot_t[:, :half], shared[:half, cc])
    for c in range(chunks // 2):
        cc = slice(c * 256, (c + 1) * 256)
        gp_ref[:, cc] = (own[:, cc] + mm(hot_t[:, half:], shared[half:, cc])).astype(BF16)

    wait_bytes(ids.at[pl.ds(0, n_dp - 1)], sent.at[0])
    wait_bytes(recv1.at[pl.ds(0, (n_dp - 1) * msg)], sent.at[1])
    wait_bytes(recv_in.at[pl.ds(0, n_y - 1)], sent.at[2])
    wait_bytes(recv_l.at[pl.ds(0, n_y - 1)], sent.at[3])
    wait_bytes(wl_all.at[pl.ds(0, n_y - 1)], sent.at[4])
    wait_bytes(recv2.at[pl.ds(0, (n_dp - 1) * msg)], sent.at[5])
    wait_bytes(wi_all.at[pl.ds(0, n_y - 1)], sent.at[6])
    wait_bytes(ls_all.at[pl.ds(0, n_y - 1)], sent.at[7])


def store(a, b, c, a_out, b_out, c_out, sems):
    copies = [
        pltpu.make_async_copy(src, dst, sems.at[k])
        for k, (src, dst) in enumerate(((a, a_out), (b, b_out), (c, c_out)))
    ]
    for copy in copies:
        copy.start()
    for copy in copies:
        copy.wait()


def per_device(z_count, queries, passages, block_lists, list_lengths, positive, loss_grad):
    n_dp, n_y = lax.axis_size("dp"), lax.axis_size("grp")
    n_blocks, shard_rows, width = passages.shape
    n_q = queries.shape[0]
    block = n_q // 2
    rows = block // n_y
    chunks = width // 128
    msg = SLOTS * chunks
    vmem = pl.BlockSpec(memory_space=pltpu.VMEM)
    hbm = pl.BlockSpec(memory_space=pltpu.HBM)
    parts = z_count // 4
    lanes = SLOTS * (n_dp // parts)
    big = (n_dp * msg, 128)
    losses, gq, gp = pl.pallas_call(
        functools.partial(kernel, z_count),
        out_shape=(
            pltpu.VMEM((2, block), F32),
            pltpu.VMEM((n_q, width), BF16),
            pltpu.VMEM((n_blocks, width), BF16),
        ),
        in_specs=[hbm] * 6,
        out_specs=(vmem, vmem, vmem),
        scratch_shapes=[
            pltpu.VMEM((n_q, width), BF16),
            pltpu.VMEM((n_blocks, width), BF16),
            pltpu.SMEM(block_lists.shape, jnp.int32),
            pltpu.SMEM(list_lengths.shape, jnp.int32),
            pltpu.VMEM((2, block), jnp.int32),
            pltpu.VMEM((2, block), F32),
            pltpu.VMEM((n_dp, 1, 128), jnp.int32),
            pltpu.VMEM(big, BF16),
            pltpu.VMEM(big, BF16),
            pltpu.VMEM(big, BF16),
            pltpu.VMEM(big, BF16),
            pltpu.VMEM(big, F32),
            pltpu.VMEM((SLOTS * n_dp, width), BF16),
            pltpu.VMEM((SLOTS * n_dp, width), BF16),
            pltpu.VMEM((n_blocks, SLOTS * n_dp), BF16),
            pltpu.VMEM((n_y, 2 * rows, n_blocks), F32),
            pltpu.VMEM((n_y, 2 * rows, n_blocks), F32),
            pltpu.VMEM((parts, n_y, rows, lanes), F32),
            pltpu.VMEM((parts, n_y, rows, lanes), F32),
            pltpu.VMEM((2 * rows, n_blocks), F32),
            pltpu.VMEM((parts, rows, lanes), F32),
            pltpu.VMEM((2, n_q, 128), F32),
            pltpu.VMEM((parts, n_y, rows, lanes), BF16),
            pltpu.VMEM((n_y, 2 * rows, n_blocks), BF16),
            pltpu.VMEM((n_y, 8, 128), F32),
            pltpu.VMEM((n_q, n_blocks), BF16),
            pltpu.VMEM((n_q, parts * lanes), BF16),
            pltpu.VMEM((parts * lanes, n_q), BF16),
            pltpu.VMEM((n_blocks, width), F32),
            pltpu.SemaphoreType.DMA((6,)),
            pltpu.SemaphoreType.DMA,
            pltpu.SemaphoreType.DMA((8,)),
            pltpu.SemaphoreType.DMA((parts,)),
            pltpu.SemaphoreType.DMA((parts,)),
            pltpu.SemaphoreType.DMA((parts,)),
            pltpu.SemaphoreType.DMA,
            pltpu.SemaphoreType.DMA((parts,)),
            pltpu.SemaphoreType.DMA((parts,)),
            pltpu.SemaphoreType.DMA,
            pltpu.SemaphoreType.DMA,
        ],
        name="loss_and_gradients",
        compiler_params=pltpu.CompilerParams(
            collective_id=0, has_side_effects=True, vmem_limit_bytes=40 * 2**20
        ),
    )(
        *(
            pltpu.with_memory_space_constraint(x, pltpu.HBM)
            for x in (
                queries,
                passages.reshape(n_blocks * shard_rows, width),
                block_lists,
                list_lengths,
                positive.reshape(2, block),
                loss_grad.reshape(2, block),
            )
        )
    )
    losses, gq, gp = pl.pallas_call(
        store,
        out_shape=tuple(jax.ShapeDtypeStruct(x.shape, x.dtype) for x in (losses, gq, gp)),
        in_specs=[vmem] * 3,
        out_specs=(hbm,) * 3,
        scratch_shapes=[pltpu.SemaphoreType.DMA((3,))],
        name="store",
    )(*(pltpu.with_memory_space_constraint(x, pltpu.VMEM) for x in (losses, gq, gp)))
    return losses.reshape(n_q), gq, gp.reshape(passages.shape)


def solution(mesh):
    in_specs = (P("dp", "grp"), P(None, "dp", "grp"), P("dp", None), P("dp"), P("dp"), P("dp"))
    out_specs = (P("dp"), P("dp", "grp"), P(None, "dp", "grp"))
    z_count = mesh.shape["dp"] // 8
    return jax.shard_map(
        functools.partial(per_device, z_count),
        mesh=mesh, in_specs=in_specs, out_specs=out_specs, check_vma=False,
    )
```

time: 146 us -> 133 us (0.911)
  Pallas kernels: 140 us -> 132 us
  local copies, waits for them, and re-layouts: 4.91 us -> 0 us
    pallas_call x1 -> x2, Pallas kernels: 140 us -> 132 us  [the longest x1 131 us: per_device(): pl.pallas_call(functools.partial(kernel, z_count), out_shape=(pltpu.VMEM(...]
    unnamed x15 -> x0, local copies, waits for them, and re-layouts: 4.91 us -> none
where the time goes in v2:
time: 133 us; the launch traced here: 132 us
  Pallas kernels  132 us (99%)
    pallas_call x1, Pallas kernels, per_device(): pl.pallas_call(functools.partial(kernel, z_count), out_shape=(pltpu.VMEM(...  131 us

profile of v2, /device:TPU:1, one launch (start us, length us, event | category | flops | bytes accessed | tf_op | source)
XLA Modules:
  0.0 132.5 jit_solution(15736880603989901262)
XLA Ops:
  0.6 130.8 %loss_and_gradients.1 = (f32[2,128]{1,0:T(2,128)S(1)}, bf16[256,1024]{1,0:T(8,128)(2,1)S(1)}, bf16[256,1024]{1,0:T(8,128)(2,1)S(1)}) custom-call(bf16[256,1024]{1,0:T(8,128)(2,1)} %q_hbm.1, bf16[256,1024]{1,0:T(8,128)(2,1)} %bitcast.5, s32[2,3]{1,0:T(2,128)} %lists_hbm.1, s32[2]{0:T(128)} %lens_hbm.1, s32[2,128]{1,0:T(2,128)} %bitcast.6, f32[2,128]{1,0:T(2,128)} %bitcast.7), custom_call_target="tpu_custom_call" | custom-call | tf_op jit(solution)/shard_map/loss_and_gradients/pallas_call | solution.py:369
  131.5 1.0 store.1

commit v3 on v2

v3 whole, which is shorter than its diff:
```python
import functools
import math

import jax
import jax.numpy as jnp
from jax import lax
from jax.experimental import pallas as pl
from jax.experimental.pallas import tpu as pltpu
from jax.sharding import PartitionSpec as P

D = 4096
SCALE = 3.0 / math.sqrt(D)
SLOTS = 4
LOGICAL = pl.DeviceIdType.LOGICAL
NN = (((1,), (0,)), ((), ()))
NT = (((1,), (1,)), ((), ()))
F32, BF16 = jnp.float32, jnp.bfloat16


def mm(a, b, dims=NN):
    return lax.dot_general(a, b, dims, preferred_element_type=F32)


def kernel(
    z_count,
    q_hbm, p_hbm, lists_hbm, lens_hbm, pos_hbm, lg_hbm,
    loss_ref, gq_ref, gp_ref,
    q_ref, p_ref, lists_ref, lens_ref, pos_ref, lg_ref,
    ids, send1, recv1, send2a, recv2a, send2b, recv2b, send2c, recv2c, wide, listed, shared, hot_t,
    part_in, recv_in, part_l, recv_l, sum_in, sum_l, cols,
    wl_all, wi_all, ls_all, w_in, w_full, w_full_t, own,
    in_s, loc, sent, ids_r, e1_r, e2_r, e2c_r, ri_r, rl_r, al_r, ai_r, ls_r,
):
    me = lax.axis_index("dp")
    y = lax.axis_index("grp")
    n_dp = lax.axis_size("dp")
    n_y = lax.axis_size("grp")
    plane = n_dp // z_count
    my_z, my_xc = me // plane, me % plane
    block = q_ref.shape[0] // 2
    rows = block // n_y
    chunks = q_ref.shape[1] // 128
    pair = 2 * chunks
    far = z_count // 2
    order = [far, far - 1, 1 - far, 0]
    for h in range(far - 2, 0, -1):
        order += [h, -h]
    opposite = [order.index(-dz) if -dz in order else order.index(dz) for dz in order]
    parts = z_count // 4
    peers = 4 * plane
    zs = [lax.rem(my_z + dz + z_count, z_count) for dz in order]
    base = [z * (plane * n_y) + y for z in zs]
    my_part = order.index(0) // 4
    my_place = order.index(0) * plane + my_xc
    first_out = [2, 0, 1, 3] if parts == 4 else list(range(parts))

    def copy_to(src, dst, ss, rs, dev):
        return pltpu.make_async_remote_copy(
            src_ref=src, dst_ref=dst, send_sem=ss, recv_sem=rs, device_id=dev, device_id_type=LOGICAL
        )

    def wait_bytes(ref, sem):
        pltpu.make_async_copy(ref, ref, sem).wait()

    def y_peers(body):
        for k in range(1, n_y):
            g = lax.rem(y + k, n_y)
            body(g, me * n_y + g)

    def part_peers(t, body):
        def step(k, carry):
            xc = lax.rem(my_xc + k, plane)
            for i in range(4 * t, 4 * t + 4):
                body(i * plane + xc, opposite[i] * plane + my_xc, base[i] + xc * n_y)
            return carry

        lax.fori_loop(1, plane, step, 0)
        for i in range(4 * t, 4 * t + 4):
            if order[i] != 0:
                body(i * plane + my_xc, opposite[i] * plane + my_xc, base[i] + my_xc * n_y)

    def part_sizes(t):
        return peers - 1 if t == my_part else peers

    barrier = pltpu.get_barrier_semaphore()

    def greet(dev):
        pl.semaphore_signal(barrier, inc=1, device_id=dev, device_id_type=LOGICAL)

    for i, dz in enumerate(order):
        if dz != 0:
            for xc in range(plane):
                greet(base[i] + xc * n_y)
    for k in range(1, plane):
        greet(base[order.index(0)] + lax.rem(my_xc + k, plane) * n_y)
    y_peers(lambda g, dev: greet(dev))

    copies_in = [
        pltpu.make_async_copy(src, dst, in_s.at[k])
        for k, (src, dst) in enumerate(
            (
                (lists_hbm, lists_ref), (lens_hbm, lens_ref), (q_hbm, q_ref),
                (p_hbm, p_ref), (pos_hbm, pos_ref), (lg_hbm, lg_ref),
            )
        )
    ]
    for c in copies_in:
        c.start()

    copies_in[0].wait()
    copies_in[1].wait()
    len0, len1 = lens_ref[0], lens_ref[1]
    swap = len1 < len0
    early = jnp.where(swap, 1, 0)
    len_a, len_b = jnp.where(swap, len1, len0), jnp.where(swap, len0, len1)
    list_a = [jnp.where(swap, lists_ref[1, k], lists_ref[0, k]) for k in range(3)]
    list_b = [jnp.where(swap, lists_ref[0, k], lists_ref[1, k]) for k in range(3)]
    lane = lax.broadcasted_iota(jnp.int32, (1, 128), 1)
    id_row = jnp.full((1, 128), -1, jnp.int32)
    rank = []
    for s in range(SLOTS):
        k = s - len_a
        id_b = jnp.where(k == 0, list_b[0], jnp.where(k == 1, list_b[1], list_b[2]))
        in_a = jnp.int32(s) < len_a
        in_b = k < len_b
        slot_id = jnp.where(in_a, list_a[min(s, 2)], jnp.where(in_b, id_b, -1))
        rank.append(jnp.where(in_a, 0, jnp.where(in_b, 1, 2)))
        id_row = jnp.where(lane == s, slot_id, id_row)
    owner = [jnp.where(r == 0, early, jnp.where(r == 1, 1 - early, 2)) for r in rank]
    ids[my_place] = id_row

    for c in copies_in[2:]:
        c.wait()
    scores = mm(q_ref[...], p_ref[...], NT)
    for g in range(n_y):
        for b in range(2):
            part_in[g, b * rows : (b + 1) * rows, :] = scores[
                b * block + g * rows : b * block + (g + 1) * rows
            ]

    pl.semaphore_wait(barrier, n_dp - 1 + n_y - 1)

    for t in first_out:
        part_peers(
            t,
            lambda i, there, dev: copy_to(
                ids.at[my_place], ids.at[there], sent.at[0], ids_r.at[t], dev
            ).start(),
        )

    def to_messages(value, first, n, size, c):
        for h in range(2):
            wide[pl.ds(first + 2 * c + h, n, stride=size), :] = value[:, h * 128 : (h + 1) * 128]

    def from_messages(dst, first, n, size, row):
        for c in range(chunks):
            dst[row : row + n, c * 128 : (c + 1) * 128] = wide[
                pl.ds(first + c, n, stride=size), :
            ].astype(BF16)

    def at_row(ref, p):
        return ref.at[pl.ds(pl.multiple_of(p * pair, pair), pair)]

    def slab(ref, h):
        return ref.at[pl.ds(h * n_dp * pair, n_dp * pair)]

    number = lax.broadcasted_iota(jnp.int32, (peers, p_ref.shape[0]), 1)
    for h in range(2):
        src, dst = slab(send1, h), slab(recv1, h)
        for t in first_out:
            if h == 0:
                wait_bytes(ids.at[pl.ds(t * peers, part_sizes(t))], ids_r.at[t])
            id_mat = ids[t * peers : (t + 1) * peers].reshape(peers, 128)
            hot = jnp.concatenate(
                [(id_mat[:, s : s + 1] == number).astype(F32) for s in (2 * h, 2 * h + 1)], axis=0
            ).astype(BF16)
            first = (h * n_dp + t * peers) * pair
            for c in range(chunks // 2):
                value = mm(hot, p_ref[:, c * 256 : (c + 1) * 256])
                for k in range(2):
                    to_messages(value[k * peers : (k + 1) * peers], first + k * chunks, peers, pair, c)
            at = slice(first, first + peers * pair)
            send1[at, :] = wide[at, :].astype(BF16)
            part_peers(
                t,
                lambda i, there, dev: copy_to(
                    at_row(src, i), at_row(dst, there), sent.at[1 + h], e1_r.at[h], dev
                ).start(),
            )
        pltpu.make_async_copy(at_row(src, my_place), at_row(dst, my_place), loc.at[h]).start()

    y_peers(lambda g, dev: copy_to(part_in.at[g], recv_in.at[y], sent.at[3], ri_r, dev).start())
    for b in range(2):
        cols[0, b * block : (b + 1) * block, :] = jnp.broadcast_to(
            lg_ref[b : b + 1, :], (block, 128)
        ).T
        column = (pos_ref[b : b + 1, :] // block).astype(F32)
        cols[1, b * block : (b + 1) * block, :] = jnp.broadcast_to(column, (block, 128)).T
    id_mat = ids[...].reshape(n_dp, 128)
    number = lax.broadcasted_iota(jnp.int32, (n_dp, p_ref.shape[0]), 1)
    for s in range(SLOTS):
        hot_t[:, s * n_dp : (s + 1) * n_dp] = (id_mat[:, s : s + 1] == number).astype(F32).T.astype(BF16)
    recv_in[y] = part_in[y]
    wait_bytes(recv_in.at[pl.ds(0, n_y - 1)], ri_r)
    total = recv_in[0]
    for g in range(1, n_y):
        total = total + recv_in[g]
    sum_in[...] = SCALE * total
    own_cols = []
    for b in range(2):
        at = pl.ds(pl.multiple_of(b * block + y * rows, rows), rows)
        own_cols.append((cols[0, at, :][:, :1], cols[1, at, :][:, :1]))

    def listed_scores(h):
        got = slab(recv1, h)
        wait_bytes(got.at[pl.ds(0, (n_dp - 1) * pair)], e1_r.at[h])
        wait_bytes(at_row(got, my_place), loc.at[h])
        at = slice(h * n_dp * pair, (h + 1) * n_dp * pair)
        wide[at, :] = recv1[at, :].astype(F32)
        for k in range(2):
            from_messages(listed, h * n_dp * pair + k * chunks, n_dp, pair, (2 * h + k) * n_dp)
        scores = mm(q_ref[...], listed[2 * h * n_dp : 2 * (h + 1) * n_dp, :], NT)
        for k in range(2):
            of_1 = jnp.full((block, n_dp), owner[2 * h + k]) == 1
            cc = slice(k * n_dp, (k + 1) * n_dp)
            mine = jnp.where(of_1, scores[block:, cc], scores[:block, cc])
            for g in range(n_y):
                part_l[h, g, k] = mine[g * rows : (g + 1) * rows]
        y_peers(
            lambda g, dev: copy_to(
                part_l.at[h, g], recv_l.at[h, y], sent.at[4], rl_r.at[h], dev
            ).start()
        )
        recv_l[h, y] = part_l[h, y]
        wait_bytes(recv_l.at[h, pl.ds(0, n_y - 1)], rl_r.at[h])
        for k in range(2):
            total = recv_l[h, 0, k]
            for g in range(1, n_y):
                total = total + recv_l[h, g, k]
            sum_l[2 * h + k] = SCALE * total

    def pick(which, a, b):
        return jnp.where(jnp.full(a.shape, which) == 1, b, a)

    def log_total(r, slots):
        blk = early if r == 0 else 1 - early
        sc = pick(blk, sum_in[:rows, :], sum_in[rows:, :])
        opened = [
            jnp.where(jnp.full((rows, n_dp), rank[s]) == r, sum_l[s], -jnp.inf) for s in slots
        ]
        best = opened[0]
        for o in opened[1:]:
            best = jnp.maximum(best, o)
        top = jnp.maximum(
            jnp.max(sc, axis=1, keepdims=True), jnp.max(best, axis=1, keepdims=True)
        )
        terms = jnp.exp(opened[0] - top)
        for o in opened[1:]:
            terms = terms + jnp.exp(o - top)
        acc = jnp.sum(jnp.exp(sc - top), axis=1, keepdims=True) + jnp.sum(
            terms, axis=1, keepdims=True
        )
        return top + jnp.log(acc)

    grads = [
        pick(early, own_cols[0][0], own_cols[1][0]),
        pick(1 - early, own_cols[0][0], own_cols[1][0]),
    ]

    def listed_weights(s, logs):
        log_s = pick(rank[s], logs[0], logs[-1])
        grad_s = pick(rank[s], grads[0], grads[1])
        weight = grad_s * jnp.exp(sum_l[s] - log_s)
        weight = jnp.where(jnp.full((rows, n_dp), rank[s]) == 2, 0.0, weight)
        wl_all[s, y] = weight.astype(BF16)
        y_peers(
            lambda g, dev: copy_to(
                wl_all.at[s, y], wl_all.at[s, y], sent.at[5], al_r.at[s], dev
            ).start()
        )

    def shares(s, first, size):
        wait_bytes(wl_all.at[s, pl.ds(0, n_y - 1)], al_r.at[s])
        w_s = jnp.concatenate([wl_all[s, g].astype(F32) for g in range(n_y)], axis=0)
        for b in range(2):
            w_b = jnp.where(jnp.full((block, n_dp), owner[s]) == b, w_s, 0.0)
            w_full[b * block : (b + 1) * block, s * n_dp : (s + 1) * n_dp] = w_b.astype(BF16)
            w_full_t[s * n_dp : (s + 1) * n_dp, b * block : (b + 1) * block] = w_b.T.astype(BF16)
        for c in range(chunks // 2):
            share = mm(
                w_full_t[s * n_dp : (s + 1) * n_dp, :], q_ref[:, c * 256 : (c + 1) * 256]
            )
            to_messages(SCALE * share, first, n_dp, size, c)

    def send_slot(src, dst, ss, rs, own_sem):
        src[...] = wide[: n_dp * chunks, :].reshape(n_dp, chunks, 128).astype(BF16)
        for t in range(parts):
            part_peers(
                t,
                lambda i, there, dev: copy_to(src.at[i], dst.at[there], ss, rs, dev).start(),
            )
        pltpu.make_async_copy(src.at[my_place], dst.at[my_place], own_sem).start()

    listed_scores(0)
    log_a = log_total(0, (0, 1))
    listed_weights(0, (log_a,))
    shares(0, 0, chunks)
    wait_bytes(slab(recv1, 0).at[pl.ds(0, (n_dp - 1) * pair)], sent.at[1])
    wait_bytes(slab(recv1, 1).at[pl.ds(0, (n_dp - 1) * pair)], sent.at[2])
    send_slot(send2a, recv2a, sent.at[6], e2_r.at[0], loc.at[2])

    listed_scores(1)
    log_b = log_total(1, (1, 2, 3))
    for s in range(1, SLOTS):
        listed_weights(s, (log_a, log_b))
    shares(1, 0, chunks)
    send_slot(send2b, recv2b, sent.at[7], e2_r.at[1], loc.at[3])
    shares(2, 0, pair)
    shares(3, chunks, pair)
    send2c[...] = wide[: n_dp * pair, :].astype(BF16)
    for t in range(parts):
        part_peers(
            t,
            lambda i, there, dev: copy_to(
                at_row(send2c, i), at_row(recv2c, there), sent.at[8], e2c_r.at[t], dev
            ).start(),
        )
    pltpu.make_async_copy(at_row(send2c, my_place), at_row(recv2c, my_place), loc.at[4]).start()

    number_in = lax.broadcasted_iota(jnp.int32, (rows, p_ref.shape[0]), 1).astype(F32)
    ls_all[y] = jnp.zeros((8, 128), F32)
    for b in range(2):
        log_q = pick(early, log_a, log_b) if b == 0 else pick(early, log_b, log_a)
        sc = sum_in[b * rows : (b + 1) * rows, :]
        positive = number_in == own_cols[b][1]
        loss = log_q - jnp.sum(jnp.where(positive, sc, 0.0), axis=1, keepdims=True)
        weight = own_cols[b][0] * (jnp.exp(sc - log_q) - positive.astype(F32))
        wi_all[y, b * rows : (b + 1) * rows, :] = weight.astype(BF16)
        place = lax.broadcasted_iota(jnp.int32, (rows, 128), 1) - y * rows
        diag = place == lax.broadcasted_iota(jnp.int32, (rows, 128), 0)
        ls_all[y, b : b + 1, :] = jnp.sum(jnp.where(diag, loss, 0.0), axis=0, keepdims=True)
    y_peers(lambda g, dev: copy_to(wi_all.at[y], wi_all.at[y], sent.at[9], ai_r, dev).start())
    y_peers(lambda g, dev: copy_to(ls_all.at[y], ls_all.at[y], sent.at[10], ls_r, dev).start())
    wait_bytes(wi_all.at[pl.ds(0, n_y - 1)], ai_r)
    wait_bytes(ls_all.at[pl.ds(0, n_y - 1)], ls_r)
    loss_all = ls_all[0]
    for g in range(1, n_y):
        loss_all = loss_all + ls_all[g]
    loss_ref[...] = loss_all[0:2, :]
    for b in range(2):
        for g in range(n_y):
            w_in[b * block + g * rows : b * block + (g + 1) * rows, :] = wi_all[
                g, b * rows : (b + 1) * rows, :
            ]
    w_in_t = w_in[...].astype(F32).T.astype(BF16)
    for c in range(chunks // 2):
        cc = slice(c * 256, (c + 1) * 256)
        grad = mm(w_in[...], p_ref[:, cc]) + mm(w_full[...], listed[:, cc])
        gq_ref[:, cc] = (SCALE * grad).astype(BF16)
        own[:, cc] = SCALE * mm(w_in_t, q_ref[:, cc])

    for s, (src, own_sem) in enumerate(((recv2a, loc.at[2]), (recv2b, loc.at[3]))):
        wait_bytes(src.at[pl.ds(0, n_dp - 1)], e2_r.at[s])
        wait_bytes(src.at[my_place], own_sem)
        wide[: n_dp * chunks, :] = src[...].astype(F32).reshape(n_dp * chunks, 128)
        from_messages(shared, 0, n_dp, chunks, s * n_dp)
        for c in range(chunks // 2):
            cc = slice(c * 256, (c + 1) * 256)
            own[:, cc] += mm(
                hot_t[:, s * n_dp : (s + 1) * n_dp], shared[s * n_dp : (s + 1) * n_dp, cc]
            )
    for t in range(parts):
        wait_bytes(recv2c.at[pl.ds(t * peers * pair, part_sizes(t) * pair)], e2c_r.at[t])
        if t == my_part:
            wait_bytes(at_row(recv2c, my_place), loc.at[4])
        at = slice(t * peers * pair, (t + 1) * peers * pair)
        wide[at, :] = recv2c[at, :].astype(F32)
        for k in range(2):
            from_messages(
                shared, t * peers * pair + k * chunks, peers, pair, (2 + k) * n_dp + t * peers
            )
    for c in range(chunks // 2):
        cc = slice(c * 256, (c + 1) * 256)
        total = own[:, cc] + mm(hot_t[:, 2 * n_dp :], shared[2 * n_dp :, cc])
        gp_ref[:, cc] = total.astype(BF16)

    wait_bytes(ids.at[pl.ds(0, n_dp - 1)], sent.at[0])
    wait_bytes(recv_in.at[pl.ds(0, n_y - 1)], sent.at[3])
    wait_bytes(recv_l.at[:, pl.ds(0, n_y - 1)], sent.at[4])
    wait_bytes(wl_all.at[:, pl.ds(0, n_y - 1)], sent.at[5])
    wait_bytes(recv2a.at[pl.ds(0, n_dp - 1)], sent.at[6])
    wait_bytes(recv2b.at[pl.ds(0, n_dp - 1)], sent.at[7])
    wait_bytes(recv2c.at[pl.ds(0, (n_dp - 1) * pair)], sent.at[8])
    wait_bytes(wi_all.at[pl.ds(0, n_y - 1)], sent.at[9])
    wait_bytes(ls_all.at[pl.ds(0, n_y - 1)], sent.at[10])


def store(a, b, c, a_out, b_out, c_out, sems):
    copies = [
        pltpu.make_async_copy(src, dst, sems.at[k])
        for k, (src, dst) in enumerate(((a, a_out), (b, b_out), (c, c_out)))
    ]
    for copy in copies:
        copy.start()
    for copy in copies:
        copy.wait()


def per_device(z_count, queries, passages, block_lists, list_lengths, positive, loss_grad):
    n_dp, n_y = lax.axis_size("dp"), lax.axis_size("grp")
    n_blocks, shard_rows, width = passages.shape
    n_q = queries.shape[0]
    block = n_q // 2
    rows = block // n_y
    chunks = width // 128
    msg = SLOTS * chunks
    vmem = pl.BlockSpec(memory_space=pltpu.VMEM)
    hbm = pl.BlockSpec(memory_space=pltpu.HBM)
    parts = z_count // 4
    big = (n_dp * msg, 128)
    losses, gq, gp = pl.pallas_call(
        functools.partial(kernel, z_count),
        out_shape=(
            pltpu.VMEM((2, block), F32),
            pltpu.VMEM((n_q, width), BF16),
            pltpu.VMEM((n_blocks, width), BF16),
        ),
        in_specs=[hbm] * 6,
        out_specs=(vmem, vmem, vmem),
        scratch_shapes=[
            pltpu.VMEM((n_q, width), BF16),
            pltpu.VMEM((n_blocks, width), BF16),
            pltpu.SMEM(block_lists.shape, jnp.int32),
            pltpu.SMEM(list_lengths.shape, jnp.int32),
            pltpu.VMEM((2, block), jnp.int32),
            pltpu.VMEM((2, block), F32),
            pltpu.VMEM((n_dp, 1, 128), jnp.int32),
            pltpu.VMEM(big, BF16),
            pltpu.VMEM(big, BF16),
            pltpu.VMEM((n_dp, chunks, 128), BF16),
            pltpu.VMEM((n_dp, chunks, 128), BF16),
            pltpu.VMEM((n_dp, chunks, 128), BF16),
            pltpu.VMEM((n_dp, chunks, 128), BF16),
            pltpu.VMEM((n_dp * 2 * chunks, 128), BF16),
            pltpu.VMEM((n_dp * 2 * chunks, 128), BF16),
            pltpu.VMEM(big, F32),
            pltpu.VMEM((SLOTS * n_dp, width), BF16),
            pltpu.VMEM((SLOTS * n_dp, width), BF16),
            pltpu.VMEM((n_blocks, SLOTS * n_dp), BF16),
            pltpu.VMEM((n_y, 2 * rows, n_blocks), F32),
            pltpu.VMEM((n_y, 2 * rows, n_blocks), F32),
            pltpu.VMEM((2, n_y, 2, rows, n_dp), F32),
            pltpu.VMEM((2, n_y, 2, rows, n_dp), F32),
            pltpu.VMEM((2 * rows, n_blocks), F32),
            pltpu.VMEM((SLOTS, rows, n_dp), F32),
            pltpu.VMEM((2, n_q, 128), F32),
            pltpu.VMEM((SLOTS, n_y, rows, n_dp), BF16),
            pltpu.VMEM((n_y, 2 * rows, n_blocks), BF16),
            pltpu.VMEM((n_y, 8, 128), F32),
            pltpu.VMEM((n_q, n_blocks), BF16),
            pltpu.VMEM((n_q, SLOTS * n_dp), BF16),
            pltpu.VMEM((SLOTS * n_dp, n_q), BF16),
            pltpu.VMEM((n_blocks, width), F32),
            pltpu.SemaphoreType.DMA((6,)),
            pltpu.SemaphoreType.DMA((5,)),
            pltpu.SemaphoreType.DMA((11,)),
            pltpu.SemaphoreType.DMA((parts,)),
            pltpu.SemaphoreType.DMA((2,)),
            pltpu.SemaphoreType.DMA((2,)),
            pltpu.SemaphoreType.DMA((parts,)),
            pltpu.SemaphoreType.DMA,
            pltpu.SemaphoreType.DMA((2,)),
            pltpu.SemaphoreType.DMA((SLOTS,)),
            pltpu.SemaphoreType.DMA,
            pltpu.SemaphoreType.DMA,
        ],
        name="loss_and_gradients",
        compiler_params=pltpu.CompilerParams(
            collective_id=0, has_side_effects=True, vmem_limit_bytes=40 * 2**20
        ),
    )(
        *(
            pltpu.with_memory_space_constraint(x, pltpu.HBM)
            for x in (
                queries,
                passages.reshape(n_blocks * shard_rows, width),
                block_lists,
                list_lengths,
                positive.reshape(2, block),
                loss_grad.reshape(2, block),
            )
        )
    )
    losses, gq, gp = pl.pallas_call(
        store,
        out_shape=tuple(jax.ShapeDtypeStruct(x.shape, x.dtype) for x in (losses, gq, gp)),
        in_specs=[vmem] * 3,
        out_specs=(hbm,) * 3,
        scratch_shapes=[pltpu.SemaphoreType.DMA((3,))],
        name="store",
    )(*(pltpu.with_memory_space_constraint(x, pltpu.VMEM) for x in (losses, gq, gp)))
    return losses.reshape(n_q), gq, gp.reshape(passages.shape)


def solution(mesh):
    in_specs = (P("dp", "grp"), P(None, "dp", "grp"), P("dp", None), P("dp"), P("dp"), P("dp"))
    out_specs = (P("dp"), P("dp", "grp"), P(None, "dp", "grp"))
    z_count = mesh.shape["dp"] // 8
    return jax.shard_map(
        functools.partial(per_device, z_count),
        mesh=mesh, in_specs=in_specs, out_specs=out_specs, check_vma=False,
    )
```

time: 133 us -> 121 us (0.910)
  Pallas kernels: 132 us -> 120 us
    pallas_call x1, Pallas kernels: 131 us -> 119 us  [per_device(): pl.pallas_call(functools.partial(kernel, z_count), out_shape=(pltpu.VMEM(...]
where the time goes in v3:
time: 121 us
  Pallas kernels  120 us (99%)
    pallas_call x1, Pallas kernels, per_device(): pl.pallas_call(functools.partial(kernel, z_count), out_shape=(pltpu.VMEM(...  119 us

profile of v3, /device:TPU:1, one launch (start us, length us, event | category | flops | bytes accessed | tf_op | source)
XLA Modules:
  0.0 121.0 jit_solution(12927296236640014102)
XLA Ops:
  0.6 119.3 %loss_and_gradients.1 = (f32[2,128]{1,0:T(2,128)S(1)}, bf16[256,1024]{1,0:T(8,128)(2,1)S(1)}, bf16[256,1024]{1,0:T(8,128)(2,1)S(1)}) custom-call(bf16[256,1024]{1,0:T(8,128)(2,1)} %q_hbm.1, bf16[256,1024]{1,0:T(8,128)(2,1)} %bitcast.5, s32[2,3]{1,0:T(2,128)} %lists_hbm.1, s32[2]{0:T(128)} %lens_hbm.1, s32[2,128]{1,0:T(2,128)} %bitcast.6, f32[2,128]{1,0:T(2,128)} %bitcast.7), custom_call_target="tpu_custom_call" | custom-call | tf_op jit(solution)/shard_map/loss_and_gradients/pallas_call | solution.py:421
  120.0 1.0 store.1

commit v4 on v3

--- a/solution.py
+++ b/solution.py
@@ -82,6 +82,18 @@
     def part_sizes(t):
         return peers - 1 if t == my_part else peers
 
+    copies_in = [
+        pltpu.make_async_copy(src, dst, in_s.at[k])
+        for k, (src, dst) in enumerate(
+            (
+                (lists_hbm, lists_ref), (lens_hbm, lens_ref), (q_hbm, q_ref),
+                (p_hbm, p_ref), (pos_hbm, pos_ref), (lg_hbm, lg_ref),
+            )
+        )
+    ]
+    for c in copies_in[:2]:
+        c.start()
+
     barrier = pltpu.get_barrier_semaphore()
 
     def greet(dev):
@@ -94,18 +106,9 @@
     for k in range(1, plane):
         greet(base[order.index(0)] + lax.rem(my_xc + k, plane) * n_y)
     y_peers(lambda g, dev: greet(dev))
-
-    copies_in = [
-        pltpu.make_async_copy(src, dst, in_s.at[k])
-        for k, (src, dst) in enumerate(
-            (
-                (lists_hbm, lists_ref), (lens_hbm, lens_ref), (q_hbm, q_ref),
-                (p_hbm, p_ref), (pos_hbm, pos_ref), (lg_hbm, lg_ref),
-            )
-        )
-    ]
-    for c in copies_in:
+    for c in copies_in[2:]:
         c.start()
+
 
     copies_in[0].wait()
     copies_in[1].wait()
@@ -129,15 +132,6 @@
     owner = [jnp.where(r == 0, early, jnp.where(r == 1, 1 - early, 2)) for r in rank]
     ids[my_place] = id_row
 
-    for c in copies_in[2:]:
-        c.wait()
-    scores = mm(q_ref[...], p_ref[...], NT)
-    for g in range(n_y):
-        for b in range(2):
-            part_in[g, b * rows : (b + 1) * rows, :] = scores[
-                b * block + g * rows : b * block + (g + 1) * rows
-            ]
-
     pl.semaphore_wait(barrier, n_dp - 1 + n_y - 1)
 
     for t in first_out:
@@ -164,6 +158,7 @@
     def slab(ref, h):
         return ref.at[pl.ds(h * n_dp * pair, n_dp * pair)]
 
+    copies_in[3].wait()
     number = lax.broadcasted_iota(jnp.int32, (peers, p_ref.shape[0]), 1)
     for h in range(2):
         src, dst = slab(send1, h), slab(recv1, h)
@@ -189,6 +184,15 @@
             )
         pltpu.make_async_copy(at_row(src, my_place), at_row(dst, my_place), loc.at[h]).start()
 
+    copies_in[2].wait()
+    for c in copies_in[4:]:
+        c.wait()
+    scores = mm(q_ref[...], p_ref[...], NT)
+    for g in range(n_y):
+        for b in range(2):
+            part_in[g, b * rows : (b + 1) * rows, :] = scores[
+                b * block + g * rows : b * block + (g + 1) * rows
+            ]
     y_peers(lambda g, dev: copy_to(part_in.at[g], recv_in.at[y], sent.at[3], ri_r, dev).start())
     for b in range(2):
         cols[0, b * block : (b + 1) * block, :] = jnp.broadcast_to(

time: 121 us -> 121 us (level)
  no operation moved by 1% of the time
where the time goes in v4:
time: 121 us
  Pallas kernels  120 us (99%)
    pallas_call x1, Pallas kernels, per_device(): pl.pallas_call(functools.partial(kernel, z_count), out_shape=(pltpu.VMEM(...  119 us

profile of v4, /device:TPU:1, one launch (start us, length us, event | category | flops | bytes accessed | tf_op | source)
XLA Modules:
  0.0 121.0 jit_solution(4325752702446382752)
XLA Ops:
  0.6 119.4 %loss_and_gradients.1 = (f32[2,128]{1,0:T(2,128)S(1)}, bf16[256,1024]{1,0:T(8,128)(2,1)S(1)}, bf16[256,1024]{1,0:T(8,128)(2,1)S(1)}) custom-call(bf16[256,1024]{1,0:T(8,128)(2,1)} %q_hbm.1, bf16[256,1024]{1,0:T(8,128)(2,1)} %bitcast.5, s32[2,3]{1,0:T(2,128)} %lists_hbm.1, s32[2]{0:T(128)} %lens_hbm.1, s32[2,128]{1,0:T(2,128)} %bitcast.6, f32[2,128]{1,0:T(2,128)} %bitcast.7), custom_call_target="tpu_custom_call" | custom-call | tf_op jit(solution)/shard_map/loss_and_gradients/pallas_call | solution.py:425
  120.0 1.0 store.1

commit v5 on v4

--- a/solution.py
+++ b/solution.py
@@ -91,7 +91,7 @@
             )
         )
     ]
-    for c in copies_in[:2]:
+    for c in copies_in:
         c.start()
 
     barrier = pltpu.get_barrier_semaphore()
@@ -106,9 +106,6 @@
     for k in range(1, plane):
         greet(base[order.index(0)] + lax.rem(my_xc + k, plane) * n_y)
     y_peers(lambda g, dev: greet(dev))
-    for c in copies_in[2:]:
-        c.start()
-
 
     copies_in[0].wait()
     copies_in[1].wait()
@@ -132,6 +129,15 @@
     owner = [jnp.where(r == 0, early, jnp.where(r == 1, 1 - early, 2)) for r in rank]
     ids[my_place] = id_row
 
+    for c in copies_in[2:]:
+        c.wait()
+    scores = mm(q_ref[...], p_ref[...], NT)
+    for g in range(n_y):
+        for b in range(2):
+            part_in[g, b * rows : (b + 1) * rows, :] = scores[
+                b * block + g * rows : b * block + (g + 1) * rows
+            ]
+
     pl.semaphore_wait(barrier, n_dp - 1 + n_y - 1)
 
     for t in first_out:
@@ -158,7 +164,6 @@
     def slab(ref, h):
         return ref.at[pl.ds(h * n_dp * pair, n_dp * pair)]
 
-    copies_in[3].wait()
     number = lax.broadcasted_iota(jnp.int32, (peers, p_ref.shape[0]), 1)
     for h in range(2):
         src, dst = slab(send1, h), slab(recv1, h)
@@ -184,15 +189,6 @@
             )
         pltpu.make_async_copy(at_row(src, my_place), at_row(dst, my_place), loc.at[h]).start()
 
-    copies_in[2].wait()
-    for c in copies_in[4:]:
-        c.wait()
-    scores = mm(q_ref[...], p_ref[...], NT)
-    for g in range(n_y):
-        for b in range(2):
-            part_in[g, b * rows : (b + 1) * rows, :] = scores[
-                b * block + g * rows : b * block + (g + 1) * rows
-            ]
     y_peers(lambda g, dev: copy_to(part_in.at[g], recv_in.at[y], sent.at[3], ri_r, dev).start())
     for b in range(2):
         cols[0, b * block : (b + 1) * block, :] = jnp.broadcast_to(

time: 121 us -> 121 us (level)
  no operation moved by 1% of the time
where the time goes in v5:
time: 121 us
  Pallas kernels  120 us (99%)
    pallas_call x1, Pallas kernels, per_device(): pl.pallas_call(functools.partial(kernel, z_count), out_shape=(pltpu.VMEM(...  119 us

profile of v5, /device:TPU:1, one launch (start us, length us, event | category | flops | bytes accessed | tf_op | source)
XLA Modules:
  0.0 121.0 jit_solution(16193219768149691819)
XLA Ops:
  0.6 119.3 %loss_and_gradients.1 = (f32[2,128]{1,0:T(2,128)S(1)}, bf16[256,1024]{1,0:T(8,128)(2,1)S(1)}, bf16[256,1024]{1,0:T(8,128)(2,1)S(1)}) custom-call(bf16[256,1024]{1,0:T(8,128)(2,1)} %q_hbm.1, bf16[256,1024]{1,0:T(8,128)(2,1)} %bitcast.5, s32[2,3]{1,0:T(2,128)} %lists_hbm.1, s32[2]{0:T(128)} %lens_hbm.1, s32[2,128]{1,0:T(2,128)} %bitcast.6, f32[2,128]{1,0:T(2,128)} %bitcast.7), custom_call_target="tpu_custom_call" | custom-call | tf_op jit(solution)/shard_map/loss_and_gradients/pallas_call | solution.py:421
  120.0 1.0 store.1
